TPU v7x, 128 devices: a whole 4x4x4 slice. The times are simulated.
128 devices in a mesh: visit: 8 (over y, core), patch: 16 (over z, x).
Axes of the slice: x: 4, y: 4, z: 4, core: 2. Of those that a mesh axis runs over, the one named last changes fastest.
Arguments:
- image: float32 [4096, 128, 128], P(('visit', 'patch')), may hold values from -8 to 8
- weight: float32 [4096, 128, 128], P(('visit', 'patch')), may hold values from 0.25 to 4
- coeffs: float32 [4096, 16], P(('visit', 'patch')), may hold values from -3 to 3
- trim: int32 [4096, 4], P(('visit', 'patch')), may hold values from 0 to 31
- destination: int32 [4096], P(('visit', 'patch')), may hold values from 0 to 1023, as said below
- row_taps: float32 [16, 21], replicated, may hold values from -1 to 1
- col_taps: float32 [16, 21], replicated, may hold values from -1 to 1
Outputs:
- coadd: float32 [1024, 128, 128], P(('visit', 'patch'))
Inputs may be any that keep to these rules, and one draw needn't show every extreme that they name: `destination`: entries n * 32 to (n + 1) * 32 - 1 belong to device n; of those, at most 5 name output tiles t of one column (t // 8) % 16, and on every device some column gets exactly 5.
All inputs are finite; a program needn't handle non-finite values.
Results may differ from a plain program's by a relative error of at most 0.00011.
Values sent between devices are 32-bit elements; how exact they have to be, the bound alone decides.
A program may use at most 128 MiB of HBM per device.

v0:
```python
import jax
import jax.numpy as jnp
from jax import lax
from jax.sharding import PartitionSpec as P

TILES_DEV = 8


HIGH = lax.Precision.HIGHEST


def band_tables(taps, size):
    rows = lax.broadcasted_iota(jnp.int32, (size, size), 0)
    cols = lax.broadcasted_iota(jnp.int32, (size, size), 1)
    offset = cols - rows + taps.shape[1] // 2
    total = jnp.zeros((taps.shape[0], size, size), jnp.float32)
    for index in range(taps.shape[1]):
        total = total + jnp.where(offset == index, 1.0, 0.0)[None] * taps[:, index][:, None, None]
    return total


def match_tiles(tiles, weights, row_band, col_band):

    def one(parts):
        pixels, factors = parts
        across = jnp.einsum("ij,klj->kil", pixels, col_band, precision=HIGH)
        across = across * factors[:, None, None]
        return jnp.einsum("kmi,kil->ml", row_band, across, precision=HIGH)

    return lax.map(one, (tiles, weights), batch_size=8)


def shards(image, weight, coeffs, trim, destination, row_taps, col_taps):
    count, tile = (image.shape[0], image.shape[1])
    terms = coeffs.shape[1]
    columns = lax.axis_size("patch")
    visits = lax.axis_size("visit")
    hot_count = max(1, columns // 4)
    slots = (count // 2 + columns - 1) // columns + (
        count - count // 2 + hot_count - 1
    ) // hot_count
    row_band = band_tables(row_taps, tile)
    col_band = band_tables(col_taps, tile)
    pixel = jnp.arange(tile, dtype=jnp.int32)
    rows_in = (pixel[None, :] >= trim[:, 0:1]) & (pixel[None, :] < tile - trim[:, 1:2])
    cols_in = (pixel[None, :] >= trim[:, 2:3]) & (pixel[None, :] < tile - trim[:, 3:4])
    kept = jnp.where(rows_in[:, :, None] & cols_in[:, None, :], weight, jnp.zeros_like(weight))
    column = destination // TILES_DEV % columns
    local_row = destination // (TILES_DEV * columns) * TILES_DEV + destination % TILES_DEV
    order = jnp.arange(count, dtype=jnp.int32)
    earlier = (column[:, None] == column[None, :]) & (order[None, :] < order[:, None])
    rank = jnp.sum(earlier.astype(jnp.int32), axis=1)
    slot = column * slots + rank
    slot_match = jnp.arange(columns * slots, dtype=jnp.int32)[:, None] == slot[None, :]
    placing = slot_match.astype(jnp.float32)
    slot_row = jnp.sum(jnp.where(slot_match, local_row[None, :] + 1, 0), axis=1) - 1
    slot_row = slot_row.reshape(columns, slots)
    payload = jnp.stack([image, kept], axis=1).reshape(count, 2 * tile * tile)
    sent = jnp.dot(placing, payload, precision=HIGH).reshape(columns, slots, 2, tile, tile)
    factor_sent = jnp.dot(placing, coeffs, precision=HIGH).reshape(columns, slots, terms)
    pixels = lax.all_to_all(sent, "patch", split_axis=0, concat_axis=0, tiled=True)
    factors = lax.all_to_all(factor_sent, "patch", split_axis=0, concat_axis=0, tiled=True)
    rows_here = lax.all_to_all(slot_row, "patch", split_axis=0, concat_axis=0, tiled=True)
    sources = pixels.shape[0]
    items = pixels.shape[1]
    matched = match_tiles(
        pixels[:, :, 0].reshape(-1, tile, tile), factors.reshape(-1, terms), row_band, col_band
    )
    matched = matched.reshape(sources, items, tile, tile)
    weights_here = pixels[:, :, 1]
    received = jnp.stack([weights_here * matched, weights_here], axis=2)
    gathering = (
        jnp.arange(visits * TILES_DEV, dtype=jnp.int32)[:, None] == rows_here.reshape(-1)[None, :]
    ).astype(jnp.float32)
    column_sum = jnp.dot(gathering, received.reshape(-1, 2 * tile * tile), precision=HIGH)
    column_sum = column_sum.reshape(visits * TILES_DEV, 2, tile, tile)
    owned = lax.psum_scatter(column_sum, "visit", scatter_dimension=0, tiled=True)
    return owned[:, 0] / (owned[:, 1] + 1.0)


def solution(mesh):
    placed = (
        P(("visit", "patch"), None, None),
        P(("visit", "patch"), None, None),
        P(("visit", "patch"), None),
        P(("visit", "patch"), None),
        P(("visit", "patch")),
        P(),
        P(),
    )
    return jax.shard_map(
        shards,
        mesh=mesh,
        in_specs=placed,
        out_specs=P(("visit", "patch"), None, None),
        check_vma=False,
    )
```

profile of v0, /device:TPU:1, one launch (start us, length us, event | category | flops | bytes accessed | tf_op | source)
XLA Modules:
  0.0 591.7 jit_solution(3695163722078157515)
XLA Ops:
  8.3 8.4 %all-to-all-start = ((s32[16,1,5]{2,1,0:T(1,128)}), s32[16,1,5]{2,1,0:T(1,128)S(1)}, u32[]{:S(2)}, u32[]{:S(2)}) async-start(s32[16,1,5]{2,1,0:T(1,128)} %bitcast), calls=%async_computation | async-start | bytes 16384 | tf_op jit(solution)/shard_map/all_to_all | solution.py:63
  26.7 6.9 %all-to-all-start.2 = ((f32[16,5,16]{2,1,0:T(8,128)}), f32[16,5,16]{2,1,0:T(8,128)S(1)}, u32[]{:S(2)}, u32[]{:S(2)}) async-start(f32[16,5,16]{2,1,0:T(8,128)} %reshape.314), calls=%async_computation.2 | async-start | bytes 131072 | tf_op jit(solution)/shard_map/all_to_all | solution.py:62
  33.6 9.2 %fusion.185 = f32[16,5,2,128,128]{4,0,3,2,1:T(8,128)S(1)} fusion(f32[2,128,128,32]{2,1,0,3:T(8,128)} %bitcast.97, s32[32]{0:T(128)S(1)} %multiply_add_fusion.1, s32[16,5]{0,1:T(8,128)S(1)} %multiply_add_fusion), kind=kOutput, calls=%fused_computation.187 | convolution fusion | flops 1006635520 | bytes 14680512 | tf_op jit(solution)/shard_map/dot_general | solution.py:59
  42.8 7.0 %copy.35 = f32[16,5,2,128,128]{4,3,2,1,0:T(8,128)} copy(f32[16,5,2,128,128]{4,0,3,2,1:T(8,128)S(1)} %fusion.185) | data formatting | bytes 20971520 | tf_op jit(solution)/shard_map/dot_general | solution.py:59
  49.9 6.9 %all-to-all-start.1 = ((f32[16,5,2,128,128]{4,3,2,1,0:T(8,128)}), f32[16,5,2,128,128]{4,3,2,1,0:T(8,128)}, u32[]{:S(2)}, u32[]{:S(2)}) async-start(f32[16,5,2,128,128]{4,3,2,1,0:T(8,128)} %copy.35), calls=%async_computation.1 | async-start | bytes 20971520 | tf_op jit(solution)/shard_map/all_to_all | solution.py:61
  59.9 148.0 %all-to-all-done.1 = f32[16,5,2,128,128]{4,3,2,1,0:T(8,128)} async-done(((f32[16,5,2,128,128]{4,3,2,1,0:T(8,128)}), f32[16,5,2,128,128]{4,3,2,1,0:T(8,128)}, u32[]{:S(2)}, u32[]{:S(2)}) %all-to-all-start.1) | async-done | bytes 10485792 | tf_op jit(solution)/shard_map/all_to_all | solution.py:61
  207.8 9.7 %fusion.250 = (f32[16,5,1,128,128]{4,3,2,1,0:T(8,128)}, f32[16,5,1,128,128]{4,3,1,0,2:T(8,128)}) fusion(f32[16,5,2,128,128]{4,3,2,1,0:T(8,128)} %all-to-all-done.1), kind=kLoop, calls=%fused_computation.322 | loop fusion | bytes 20971520 | tf_op jit(solution)/shard_map/slice | solution.py:67
  217.5 263.9 %while.12 = (s32[]{:T(128)}, f32[10,8,128,128]{3,2,1,0:T(8,128)}, f32[10,8,128,128]{3,2,1,0:T(8,128)}, f32[10,8,16]{2,1,0:T(8,128)S(1)}, f32[16]{0:T(128)S(1)}, ...) while((s32[]{:T(128)}, f32[10,8,128,128]{3,2,1,0:T(8,128)}, ...), condition=%wide.region_3.4_spmd.clone.clone, body=%wide.region_2.3_spmd.clone.clone.sunk | while | flops 6466043904 | bytes 22680264 | solution.py:30
  232.9 9.2 %fusion.262 = f32[8,128,16,128]{3,1,2,0:T(8,128)S(1)} fusion(f32[16]{0:T(128)S(1)} %get-tuple-element.1271, f32[128,128]{1,0:T(8,128)S(1)} %get-tuple-element.1272, f32[16]{0:T(128)S(1)} %get-tuple-element.1269, f32[128,128]{1,0:T(8,128)S(1)} %get-tuple-element.1270, f32[16]{0:T(128)S(1)} %get-tuple-element.1267, ...), kind=kOutput, calls=%fused_computation.8.clone.1 | convolution fusion | flops 3231973376 | bytes 10290500 | tf_op jit(solution)/shard_map/while/body/eval_jaxpr/vmap(ij,klj->kil)/dot_general | solution.py:26
  242.1 14.6 %fusion.263 = f32[1,8,128,128]{2,3,1,0:T(8,128)S(1)} fusion(f32[8,128,16,128]{3,1,2,0:T(8,128)S(1)} %fusion.262, f32[8,16]{1,0:T(8,128)S(1)} %dynamic-slice_bitcast_fusion.2, f32[16]{0:T(128)S(1)} %get-tuple-element.1293, f32[16]{0:T(128)S(1)} %get-tuple-element.1292, f32[16]{0:T(128)S(1)} %get-tuple-element.1291, f32[16]{0:T(128)S(1)} %get-tuple-element.1290, ...), kind=kOutput, calls=%fused_computation.6.clone.1 | convolution fusion | flops 3234070528 | bytes 10291008 | tf_op jit(solution)/shard_map/while/body/eval_jaxpr/vmap(kmi,kil->ml)/dot_general | solution.py:28
  257.7 9.1 %fusion.262 = f32[8,128,16,128]{3,1,2,0:T(8,128)S(1)} fusion(f32[16]{0:T(128)S(1)} %get-tuple-element.1271, f32[128,128]{1,0:T(8,128)S(1)} %get-tuple-element.1272, f32[16]{0:T(128)S(1)} %get-tuple-element.1269, f32[128,128]{1,0:T(8,128)S(1)} %get-tuple-element.1270, f32[16]{0:T(128)S(1)} %get-tuple-element.1267, ...), kind=kOutput, calls=%fused_computation.8.clone.1 | convolution fusion | flops 3231973376 | bytes 10290500 | tf_op jit(solution)/shard_map/while/body/eval_jaxpr/vmap(ij,klj->kil)/dot_general | solution.py:26
  266.9 14.6 %fusion.263 = f32[1,8,128,128]{2,3,1,0:T(8,128)S(1)} fusion(f32[8,128,16,128]{3,1,2,0:T(8,128)S(1)} %fusion.262, f32[8,16]{1,0:T(8,128)S(1)} %dynamic-slice_bitcast_fusion.2, f32[16]{0:T(128)S(1)} %get-tuple-element.1293, f32[16]{0:T(128)S(1)} %get-tuple-element.1292, f32[16]{0:T(128)S(1)} %get-tuple-element.1291, f32[16]{0:T(128)S(1)} %get-tuple-element.1290, ...), kind=kOutput, calls=%fused_computation.6.clone.1 | convolution fusion | flops 3234070528 | bytes 10291008 | tf_op jit(solution)/shard_map/while/body/eval_jaxpr/vmap(kmi,kil->ml)/dot_general | solution.py:28
  282.6 9.2 %fusion.262 = f32[8,128,16,128]{3,1,2,0:T(8,128)S(1)} fusion(f32[16]{0:T(128)S(1)} %get-tuple-element.1271, f32[128,128]{1,0:T(8,128)S(1)} %get-tuple-element.1272, f32[16]{0:T(128)S(1)} %get-tuple-element.1269, f32[128,128]{1,0:T(8,128)S(1)} %get-tuple-element.1270, f32[16]{0:T(128)S(1)} %get-tuple-element.1267, ...), kind=kOutput, calls=%fused_computation.8.clone.1 | convolution fusion | flops 3231973376 | bytes 10290500 | tf_op jit(solution)/shard_map/while/body/eval_jaxpr/vmap(ij,klj->kil)/dot_general | solution.py:26
  291.7 14.6 %fusion.263 = f32[1,8,128,128]{2,3,1,0:T(8,128)S(1)} fusion(f32[8,128,16,128]{3,1,2,0:T(8,128)S(1)} %fusion.262, f32[8,16]{1,0:T(8,128)S(1)} %dynamic-slice_bitcast_fusion.2, f32[16]{0:T(128)S(1)} %get-tuple-element.1293, f32[16]{0:T(128)S(1)} %get-tuple-element.1292, f32[16]{0:T(128)S(1)} %get-tuple-element.1291, f32[16]{0:T(128)S(1)} %get-tuple-element.1290, ...), kind=kOutput, calls=%fused_computation.6.clone.1 | convolution fusion | flops 3234070528 | bytes 10291008 | tf_op jit(solution)/shard_map/while/body/eval_jaxpr/vmap(kmi,kil->ml)/dot_general | solution.py:28
  307.4 9.2 %fusion.262 = f32[8,128,16,128]{3,1,2,0:T(8,128)S(1)} fusion(f32[16]{0:T(128)S(1)} %get-tuple-element.1271, f32[128,128]{1,0:T(8,128)S(1)} %get-tuple-element.1272, f32[16]{0:T(128)S(1)} %get-tuple-element.1269, f32[128,128]{1,0:T(8,128)S(1)} %get-tuple-element.1270, f32[16]{0:T(128)S(1)} %get-tuple-element.1267, ...), kind=kOutput, calls=%fused_computation.8.clone.1 | convolution fusion | flops 3231973376 | bytes 10290500 | tf_op jit(solution)/shard_map/while/body/eval_jaxpr/vmap(ij,klj->kil)/dot_general | solution.py:26
  316.5 14.6 %fusion.263 = f32[1,8,128,128]{2,3,1,0:T(8,128)S(1)} fusion(f32[8,128,16,128]{3,1,2,0:T(8,128)S(1)} %fusion.262, f32[8,16]{1,0:T(8,128)S(1)} %dynamic-slice_bitcast_fusion.2, f32[16]{0:T(128)S(1)} %get-tuple-element.1293, f32[16]{0:T(128)S(1)} %get-tuple-element.1292, f32[16]{0:T(128)S(1)} %get-tuple-element.1291, f32[16]{0:T(128)S(1)} %get-tuple-element.1290, ...), kind=kOutput, calls=%fused_computation.6.clone.1 | convolution fusion | flops 3234070528 | bytes 10291008 | tf_op jit(solution)/shard_map/while/body/eval_jaxpr/vmap(kmi,kil->ml)/dot_general | solution.py:28
  332.2 9.1 %fusion.262 = f32[8,128,16,128]{3,1,2,0:T(8,128)S(1)} fusion(f32[16]{0:T(128)S(1)} %get-tuple-element.1271, f32[128,128]{1,0:T(8,128)S(1)} %get-tuple-element.1272, f32[16]{0:T(128)S(1)} %get-tuple-element.1269, f32[128,128]{1,0:T(8,128)S(1)} %get-tuple-element.1270, f32[16]{0:T(128)S(1)} %get-tuple-element.1267, ...), kind=kOutput, calls=%fused_computation.8.clone.1 | convolution fusion | flops 3231973376 | bytes 10290500 | tf_op jit(solution)/shard_map/while/body/eval_jaxpr/vmap(ij,klj->kil)/dot_general | solution.py:26
  341.3 14.6 %fusion.263 = f32[1,8,128,128]{2,3,1,0:T(8,128)S(1)} fusion(f32[8,128,16,128]{3,1,2,0:T(8,128)S(1)} %fusion.262, f32[8,16]{1,0:T(8,128)S(1)} %dynamic-slice_bitcast_fusion.2, f32[16]{0:T(128)S(1)} %get-tuple-element.1293, f32[16]{0:T(128)S(1)} %get-tuple-element.1292, f32[16]{0:T(128)S(1)} %get-tuple-element.1291, f32[16]{0:T(128)S(1)} %get-tuple-element.1290, ...), kind=kOutput, calls=%fused_computation.6.clone.1 | convolution fusion | flops 3234070528 | bytes 10291008 | tf_op jit(solution)/shard_map/while/body/eval_jaxpr/vmap(kmi,kil->ml)/dot_general | solution.py:28
  357.0 9.1 %fusion.262 = f32[8,128,16,128]{3,1,2,0:T(8,128)S(1)} fusion(f32[16]{0:T(128)S(1)} %get-tuple-element.1271, f32[128,128]{1,0:T(8,128)S(1)} %get-tuple-element.1272, f32[16]{0:T(128)S(1)} %get-tuple-element.1269, f32[128,128]{1,0:T(8,128)S(1)} %get-tuple-element.1270, f32[16]{0:T(128)S(1)} %get-tuple-element.1267, ...), kind=kOutput, calls=%fused_computation.8.clone.1 | convolution fusion | flops 3231973376 | bytes 10290500 | tf_op jit(solution)/shard_map/while/body/eval_jaxpr/vmap(ij,klj->kil)/dot_general | solution.py:26
  366.2 14.6 %fusion.263 = f32[1,8,128,128]{2,3,1,0:T(8,128)S(1)} fusion(f32[8,128,16,128]{3,1,2,0:T(8,128)S(1)} %fusion.262, f32[8,16]{1,0:T(8,128)S(1)} %dynamic-slice_bitcast_fusion.2, f32[16]{0:T(128)S(1)} %get-tuple-element.1293, f32[16]{0:T(128)S(1)} %get-tuple-element.1292, f32[16]{0:T(128)S(1)} %get-tuple-element.1291, f32[16]{0:T(128)S(1)} %get-tuple-element.1290, ...), kind=kOutput, calls=%fused_computation.6.clone.1 | convolution fusion | flops 3234070528 | bytes 10291008 | tf_op jit(solution)/shard_map/while/body/eval_jaxpr/vmap(kmi,kil->ml)/dot_general | solution.py:28
  381.8 9.2 %fusion.262 = f32[8,128,16,128]{3,1,2,0:T(8,128)S(1)} fusion(f32[16]{0:T(128)S(1)} %get-tuple-element.1271, f32[128,128]{1,0:T(8,128)S(1)} %get-tuple-element.1272, f32[16]{0:T(128)S(1)} %get-tuple-element.1269, f32[128,128]{1,0:T(8,128)S(1)} %get-tuple-element.1270, f32[16]{0:T(128)S(1)} %get-tuple-element.1267, ...), kind=kOutput, calls=%fused_computation.8.clone.1 | convolution fusion | flops 3231973376 | bytes 10290500 | tf_op jit(solution)/shard_map/while/body/eval_jaxpr/vmap(ij,klj->kil)/dot_general | solution.py:26
  391.0 14.6 %fusion.263 = f32[1,8,128,128]{2,3,1,0:T(8,128)S(1)} fusion(f32[8,128,16,128]{3,1,2,0:T(8,128)S(1)} %fusion.262, f32[8,16]{1,0:T(8,128)S(1)} %dynamic-slice_bitcast_fusion.2, f32[16]{0:T(128)S(1)} %get-tuple-element.1293, f32[16]{0:T(128)S(1)} %get-tuple-element.1292, f32[16]{0:T(128)S(1)} %get-tuple-element.1291, f32[16]{0:T(128)S(1)} %get-tuple-element.1290, ...), kind=kOutput, calls=%fused_computation.6.clone.1 | convolution fusion | flops 3234070528 | bytes 10291008 | tf_op jit(solution)/shard_map/while/body/eval_jaxpr/vmap(kmi,kil->ml)/dot_general | solution.py:28
  406.6 9.1 %fusion.262 = f32[8,128,16,128]{3,1,2,0:T(8,128)S(1)} fusion(f32[16]{0:T(128)S(1)} %get-tuple-element.1271, f32[128,128]{1,0:T(8,128)S(1)} %get-tuple-element.1272, f32[16]{0:T(128)S(1)} %get-tuple-element.1269, f32[128,128]{1,0:T(8,128)S(1)} %get-tuple-element.1270, f32[16]{0:T(128)S(1)} %get-tuple-element.1267, ...), kind=kOutput, calls=%fused_computation.8.clone.1 | convolution fusion | flops 3231973376 | bytes 10290500 | tf_op jit(solution)/shard_map/while/body/eval_jaxpr/vmap(ij,klj->kil)/dot_general | solution.py:26
  415.8 14.6 %fusion.263 = f32[1,8,128,128]{2,3,1,0:T(8,128)S(1)} fusion(f32[8,128,16,128]{3,1,2,0:T(8,128)S(1)} %fusion.262, f32[8,16]{1,0:T(8,128)S(1)} %dynamic-slice_bitcast_fusion.2, f32[16]{0:T(128)S(1)} %get-tuple-element.1293, f32[16]{0:T(128)S(1)} %get-tuple-element.1292, f32[16]{0:T(128)S(1)} %get-tuple-element.1291, f32[16]{0:T(128)S(1)} %get-tuple-element.1290, ...), kind=kOutput, calls=%fused_computation.6.clone.1 | convolution fusion | flops 3234070528 | bytes 10291008 | tf_op jit(solution)/shard_map/while/body/eval_jaxpr/vmap(kmi,kil->ml)/dot_general | solution.py:28
  431.4 9.2 %fusion.262 = f32[8,128,16,128]{3,1,2,0:T(8,128)S(1)} fusion(f32[16]{0:T(128)S(1)} %get-tuple-element.1271, f32[128,128]{1,0:T(8,128)S(1)} %get-tuple-element.1272, f32[16]{0:T(128)S(1)} %get-tuple-element.1269, f32[128,128]{1,0:T(8,128)S(1)} %get-tuple-element.1270, f32[16]{0:T(128)S(1)} %get-tuple-element.1267, ...), kind=kOutput, calls=%fused_computation.8.clone.1 | convolution fusion | flops 3231973376 | bytes 10290500 | tf_op jit(solution)/shard_map/while/body/eval_jaxpr/vmap(ij,klj->kil)/dot_general | solution.py:26
  440.6 14.6 %fusion.263 = f32[1,8,128,128]{2,3,1,0:T(8,128)S(1)} fusion(f32[8,128,16,128]{3,1,2,0:T(8,128)S(1)} %fusion.262, f32[8,16]{1,0:T(8,128)S(1)} %dynamic-slice_bitcast_fusion.2, f32[16]{0:T(128)S(1)} %get-tuple-element.1293, f32[16]{0:T(128)S(1)} %get-tuple-element.1292, f32[16]{0:T(128)S(1)} %get-tuple-element.1291, f32[16]{0:T(128)S(1)} %get-tuple-element.1290, ...), kind=kOutput, calls=%fused_computation.6.clone.1 | convolution fusion | flops 3234070528 | bytes 10291008 | tf_op jit(solution)/shard_map/while/body/eval_jaxpr/vmap(kmi,kil->ml)/dot_general | solution.py:28
  456.3 9.1 %fusion.262 = f32[8,128,16,128]{3,1,2,0:T(8,128)S(1)} fusion(f32[16]{0:T(128)S(1)} %get-tuple-element.1271, f32[128,128]{1,0:T(8,128)S(1)} %get-tuple-element.1272, f32[16]{0:T(128)S(1)} %get-tuple-element.1269, f32[128,128]{1,0:T(8,128)S(1)} %get-tuple-element.1270, f32[16]{0:T(128)S(1)} %get-tuple-element.1267, ...), kind=kOutput, calls=%fused_computation.8.clone.1 | convolution fusion | flops 3231973376 | bytes 10290500 | tf_op jit(solution)/shard_map/while/body/eval_jaxpr/vmap(ij,klj->kil)/dot_general | solution.py:26
  465.4 14.6 %fusion.263 = f32[1,8,128,128]{2,3,1,0:T(8,128)S(1)} fusion(f32[8,128,16,128]{3,1,2,0:T(8,128)S(1)} %fusion.262, f32[8,16]{1,0:T(8,128)S(1)} %dynamic-slice_bitcast_fusion.2, f32[16]{0:T(128)S(1)} %get-tuple-element.1293, f32[16]{0:T(128)S(1)} %get-tuple-element.1292, f32[16]{0:T(128)S(1)} %get-tuple-element.1291, f32[16]{0:T(128)S(1)} %get-tuple-element.1290, ...), kind=kOutput, calls=%fused_computation.6.clone.1 | convolution fusion | flops 3234070528 | bytes 10291008 | tf_op jit(solution)/shard_map/while/body/eval_jaxpr/vmap(kmi,kil->ml)/dot_general | solution.py:28
  481.3 7.8 %fusion.249 = f32[16,5,1,128,128]{4,3,1,0,2:T(8,128)} fusion(f32[16,5,1,128,128]{4,3,1,0,2:T(8,128)} %bitcast.100, f32[16,5,2,128,128]{4,3,2,1,0:T(8,128)} %all-to-all-done.1), kind=kLoop, calls=%fused_computation.321 | loop fusion | flops 1310720 | bytes 15728640 | tf_op jit(solution)/shard_map/mul | solution.py:71
  498.9 11.6 %reshape.315 = f32[80,32768]{1,0:T(8,128)} reshape(f32[16,5,2,128,128]{4,3,2,1,0:T(8,128)} %copy.40) | data formatting | bytes 20971520 | tf_op jit(solution)/shard_map/reshape | solution.py:75
  516.3 11.2 %fusion.183 = f32[64,2,128,128]{3,0,2,1:T(8,128)} fusion(f32[2,128,128,80]{2,1,0,3:T(8,128)S(1)} %bitcast.95, s32[80]{0:T(128)S(1)} %eq.278), kind=kOutput, calls=%fused_computation.182 | convolution fusion | flops 2013271040 | bytes 18874688 | tf_op jit(solution)/shard_map/dot_general | solution.py:75
  527.5 54.8 %reduce-scatter.2.cloned.1.call-done = f32[8,2,128,128]{3,0,2,1:T(8,128)} async-done(((f32[64,2,128,128]{3,0,2,1:T(8,128)}), f32[8,2,128,128]{3,0,2,1:T(8,128)}) %reduce-scatter.2.cloned.1.call-update) | async-done | bytes 1048592 | tf_op jit(solution)/shard_map/reduce_scatter | solution.py:77
  (84 shorter events, 42.9 us)
Async XLA Ops:
  6.5 11.1 %copy-start = (f32[32,16]{0,1:T(8,128)S(1)}, f32[32,16]{0,1:T(8,128)}, u32[]{:S(2)}) copy-start(f32[32,16]{0,1:T(8,128)} %param.11) | copy-start | bytes 6148
  6.5 14.1 %copy-start.4 = (f32[32,128,128]{2,1,0:T(8,128)S(1)}, f32[32,128,128]{2,1,0:T(8,128)}, u32[]{:S(2)}) copy-start(f32[32,128,128]{2,1,0:T(8,128)} %param.9) | copy-start | bytes 6291460
  8.3 18.4 %all-to-all-start = ((s32[16,1,5]{2,1,0:T(1,128)}), s32[16,1,5]{2,1,0:T(1,128)S(1)}, u32[]{:S(2)}, u32[]{:S(2)}) async-start(s32[16,1,5]{2,1,0:T(1,128)} %bitcast), calls=%async_computation | async-start | bytes 16384 | tf_op jit(solution)/shard_map/all_to_all | solution.py:63
  26.7 23.2 %all-to-all-start.2 = ((f32[16,5,16]{2,1,0:T(8,128)}), f32[16,5,16]{2,1,0:T(8,128)S(1)}, u32[]{:S(2)}, u32[]{:S(2)}) async-start(f32[16,5,16]{2,1,0:T(8,128)} %reshape.314), calls=%async_computation.2 | async-start | bytes 131072 | tf_op jit(solution)/shard_map/all_to_all | solution.py:62
  49.9 7.0 %copy-start.2 = (f32[16,21]{1,0:T(8,128)S(1)}, f32[16,21]{1,0:T(8,128)}, u32[]{:S(2)}) copy-start(f32[16,21]{1,0:T(8,128)} %param.14) | copy-start | bytes 4036
  49.9 7.0 %copy-start.3 = (f32[16,21]{1,0:T(8,128)S(1)}, f32[16,21]{1,0:T(8,128)}, u32[]{:S(2)}) copy-start(f32[16,21]{1,0:T(8,128)} %param.15) | copy-start | bytes 4036
  49.9 158.0 %all-to-all-start.1 = ((f32[16,5,2,128,128]{4,3,2,1,0:T(8,128)}), f32[16,5,2,128,128]{4,3,2,1,0:T(8,128)}, u32[]{:S(2)}, u32[]{:S(2)}) async-start(f32[16,5,2,128,128]{4,3,2,1,0:T(8,128)} %copy.35), calls=%async_computation.1 | async-start | bytes 20971520 | tf_op jit(solution)/shard_map/all_to_all | solution.py:61
  56.8 525.5 %reduce-scatter.2.cloned.1.call-start = ((), (), s32[]{:S(2)}) async-start(), calls=%async_computation.4 | async-start | bytes 9437184 | tf_op jit(solution)/shard_map/reduce_scatter | solution.py:77
  527.5 57.0 %copy-start.1 = (f32[32,16]{0,1:T(8,128)S(1)}, f32[32,16]{0,1:T(8,128)}, u32[]{:S(2)}) copy-start(f32[32,16]{0,1:T(8,128)} %param.11) | copy-start | bytes 6148
Sparse Core Ops, SparseCore 0:
  527.6 54.6 reduce-scatter.1
where the time goes:
time: 597 us; the launch traced here: 592 us
  matrix products  258 us (43%)
  waiting for transfers between devices  203 us (34%)
  local copies, waits for them, and re-layouts  59.3 us (10%)
  starting transfers between devices  22.3 us (4%)
  other arithmetic  19.4 us (3%)
  loops' own time  15.8 us (3%)
  between operations  14 us (2%)
    all_to_all x1, waiting for transfers between devices, shards(): lax.all_to_all(sent, 'patch', split_axis=0, concat_axis=0, tiled=True)  148 us
    dot_general x10, matrix products, one(): return jnp.einsum('kmi,kil->ml', row_band, across, precision=HIGH)  146 us
    dot_general x10, matrix products, one(): across = jnp.einsum('ij,klj->kil', pixels, col_band, precision=HIGH)  91.6 us
    reduce_scatter x1, waiting for transfers between devices, shards(): lax.psum_scatter(column_sum, 'visit', scatter_dimension=0, tiled=True)  54.8 us
    another operation x1, loops' own time, match_tiles(): return lax.map(one, (tiles, weights), batch_size=8)  15.8 us
  transfers between devices with their start and end apart: 4, of which 2 were waited for; matrix products, arithmetic and copies ran while one was open for 5% of the time, Pallas kernels for 0%

commit v1 on v0

v1 whole, which is shorter than its diff:
```python
import jax
import jax.numpy as jnp
from jax import lax
from jax.experimental import pallas as pl
from jax.experimental.pallas import tpu as pltpu
from jax.sharding import PartitionSpec as P

MESH = pl.DeviceIdType.MESH
F32 = jnp.float32
BF16 = jnp.bfloat16
I32 = jnp.int32

TILE = 128
TAPS = 21
NB = 16
COUNT = 32
OWNED = 8
SLOTS = 5
ROWS = 32
PARTS = TILE // ROWS
CHUNKS = 2 * PARTS
WINDOW = 80
QUAD = 4

SHIFTS = (
    (0, 0),
    (2, 2),
    (1, 2), (2, 1), (3, 2), (2, 3),
    (2, 0), (0, 2),
    (1, 1), (3, 3),
    (1, 3), (3, 1),
    (0, 1), (1, 0), (0, 3), (3, 0),
)
SIDE = 4
PLANE = len(SHIFTS)


def kernel(
    perm, dest, trim, coef, rtap, ctap, img, wgt, out,
    kept, nums, rl, cc, xr, wsp, send, recv, acc, msend, mrecv, tabv, tabs,
    csend, crecv, ysend, yrecv,
    s_sem, r_sem, ms_sem, mr_sem, cs_sem, cr_sem, ys_sem, yr_sem, tab_sem,
):
    visit, patch = lax.axis_index("visit"), lax.axis_index("patch")
    y, core = visit // 2, visit % 2
    z, x = patch // SIDE, patch % SIDE

    def column(d):
        dz, dx = SHIFTS[d]
        return lax.rem(z + dz, SIDE) * SIDE + lax.rem(x + dx, SIDE)

    def in_y(dy):
        return lax.rem(y + dy, SIDE) * 2 + core

    partners = [(visit, column(d)) for d in range(1, PLANE)]
    partners += [(visit + 1 - 2 * core, patch)]
    partners += [(in_y(dy), patch) for dy in range(1, SIDE)]
    barrier = pltpu.get_barrier_semaphore()
    for partner in partners:
        pl.semaphore_signal(barrier, inc=1, device_id=partner, device_id_type=MESH)

    row_of = lax.broadcasted_iota(I32, (TILE, TILE), 0)
    lane_of = lax.broadcasted_iota(I32, (TILE, TILE), 1)

    def keep(n, _):
        inside = (row_of >= trim[n, 0]) & (row_of < TILE - trim[n, 1])
        inside &= (lane_of >= trim[n, 2]) & (lane_of < TILE - trim[n, 3])
        kept[n] = jnp.where(inside, wgt[n], 0.0)
        return 0

    lax.fori_loop(0, COUNT, keep, 0)
    kept[COUNT] = jnp.zeros((TILE, TILE), F32)
    nums[COUNT] = jnp.zeros((TILE, TILE), F32)

    sub_of = lax.broadcasted_iota(I32, (8, TILE), 0)

    def meta_copy(d):
        return pltpu.make_async_remote_copy(
            src_ref=msend.at[d], dst_ref=mrecv.at[d],
            send_sem=ms_sem.at[d], recv_sem=mr_sem.at[d],
            device_id=(visit, column(d)), device_id_type=MESH,
        )

    def plane_copy(c, d):
        return pltpu.make_async_remote_copy(
            src_ref=send.at[c, d], dst_ref=recv.at[c, d],
            send_sem=s_sem.at[c, d], recv_sem=r_sem.at[c, d],
            device_id=(visit, column(d)), device_id_type=MESH,
        )

    def plane_wait(c, d):
        return pltpu.make_async_remote_copy(
            src_ref=send.at[c, d], dst_ref=recv.at[c, d],
            send_sem=s_sem.at[c, d], recv_sem=r_sem.at[c, d],
            device_id=(visit, column(1)), device_id_type=MESH,
        )

    def core_copy(c):
        return pltpu.make_async_remote_copy(
            src_ref=csend.at[c], dst_ref=crecv.at[c],
            send_sem=cs_sem.at[c], recv_sem=cr_sem.at[c],
            device_id=(visit + 1 - 2 * core, patch), device_id_type=MESH,
        )

    def y_copy(c, dy):
        return pltpu.make_async_remote_copy(
            src_ref=ysend.at[c, dy], dst_ref=yrecv.at[c, dy],
            send_sem=ys_sem.at[c, dy], recv_sem=yr_sem.at[c, dy],
            device_id=(in_y(dy), patch), device_id_type=MESH,
        )

    for d in range(PLANE):
        rows = jnp.full((8, TILE), -1, I32)
        for k in range(SLOTS):
            n = perm[column(d) * 8 + k]
            to = dest[jnp.minimum(n, COUNT - 1)]
            row = jnp.where(n < COUNT, to // (OWNED * PLANE) * OWNED + to % OWNED, -1)
            rows = jnp.where(sub_of == k, row, rows)
        if d == 0:
            mrecv[0] = rows
        else:
            msend[d] = rows

    def fill(source, c, q, d):
        for k in range(SLOTS):
            n = perm[column(d) * 8 + k]
            block = source[n, pl.ds(q * ROWS, ROWS), :]
            target = recv if d == 0 else send
            target[c, d, k * ROWS:(k + 1) * ROWS, :] = block

    def send_part(source, first):
        def one(q, _):
            c = first + q
            for d in range(1, PLANE):
                fill(source, c, q, d)
                plane_copy(c, d).start()
            fill(source, c, q, 0)
            return 0

        return one

    pl.semaphore_wait(barrier, len(partners))
    for d in range(1, PLANE):
        meta_copy(d).start()
    lax.fori_loop(0, PARTS, send_part(kept, 0), 0)

    half_row = lax.broadcasted_iota(I32, (TILE // 2, 2 * TILE), 0)
    half_lane = lax.broadcasted_iota(I32, (TILE // 2, 2 * TILE), 1)
    piece = (half_lane >= WINDOW).astype(I32) + (half_lane >= 2 * WINDOW).astype(I32)
    place = half_lane - piece * WINDOW

    def tables(k, _):
        for h in range(2):
            offset = place + h * (TILE - WINDOW) - half_row - h * (TILE // 2) + TAPS // 2
            offset = jnp.where(half_lane < 3 * WINDOW, offset, -1)
            taps = jnp.zeros((TILE // 2, 2 * TILE), F32)
            for index in range(TAPS):
                taps = jnp.where(offset == index, rtap[k, index], taps)
            high = taps.astype(BF16).astype(F32)
            rl[h, pl.ds(k * (TILE // 2), TILE // 2), :] = jnp.where(
                piece == 2, taps - high, high
            ).astype(BF16)
        offset = row_of - lane_of + TAPS // 2
        taps = jnp.zeros((TILE, TILE), F32)
        for index in range(TAPS):
            taps = jnp.where(offset == index, ctap[k, index], taps)
        high = taps.astype(BF16)
        cc[pl.ds(k * TILE, TILE), 0:TILE] = high
        cc[pl.ds(k * TILE, TILE), TILE:] = (taps - high.astype(F32)).astype(BF16)
        return 0

    lax.fori_loop(0, NB, tables, 0)
    for h in range(2):
        xr[h, 3 * WINDOW:, :] = jnp.zeros((2 * TILE - 3 * WINDOW, 2 * TILE), BF16)

    def match(i, _):
        for pair in range(QUAD // 2):
            for u in range(2):
                pixels = img[i * QUAD + pair * 2 + u]
                high = pixels.astype(BF16)
                low = (pixels - high.astype(F32)).astype(BF16)
                lanes = slice(u * TILE, (u + 1) * TILE)
                for h in range(2):
                    a = h * (TILE - WINDOW)
                    xr[h, 0:WINDOW, lanes] = high[a:a + WINDOW]
                    xr[h, WINDOW:2 * WINDOW, lanes] = low[a:a + WINDOW]
                    xr[h, 2 * WINDOW:3 * WINDOW, lanes] = high[a:a + WINDOW]
            for h in range(2):
                for g in range(0, NB, 4):
                    down = jnp.dot(
                        rl[h, g * (TILE // 2):(g + 4) * (TILE // 2), :], xr[h],
                        preferred_element_type=F32,
                    )
                    for k in range(g, g + 4):
                        for u in range(2):
                            t = pair * 2 + u
                            b = (k - g) * (TILE // 2)
                            w = down[b:b + TILE // 2, u * TILE:(u + 1) * TILE]
                            w = w * coef[i * QUAD + t, k]
                            high = w.astype(BF16)
                            r = t * TILE + h * (TILE // 2)
                            lanes = slice(k * TILE, (k + 1) * TILE)
                            wsp[r:r + TILE // 2, lanes] = high
                            r += QUAD * TILE
                            wsp[r:r + TILE // 2, lanes] = (w - high.astype(F32)).astype(BF16)
        both = jnp.dot(wsp[...], cc[...], preferred_element_type=F32)
        both = both[:, :TILE] + both[:, TILE:]
        for t in range(QUAD):
            n = i * QUAD + t
            matched = both[t * TILE:(t + 1) * TILE]
            matched = matched + both[(QUAD + t) * TILE:(QUAD + t + 1) * TILE]
            nums[n] = kept[n] * matched
        return 0

    lax.fori_loop(0, COUNT // QUAD, match, 0)
    lax.fori_loop(0, PARTS, send_part(nums, PARTS), 0)

    for d in range(1, PLANE):
        meta_copy(d).wait_recv()
    along = mrecv[...].reshape(TILE, TILE)
    across = along.T
    before = jnp.where((along == across) & (row_of < lane_of), row_of, -1)
    before = jnp.max(before, axis=0, keepdims=True)
    last = jnp.max(jnp.where(along == lane_of, row_of, -1), axis=0, keepdims=True)
    table = jnp.where(sub_of == 0, before, last)
    tabv[...] = jnp.where(table < 0, TILE, table)
    move = pltpu.make_async_copy(tabv, tabs, tab_sem)
    move.start()
    move.wait()
    acc[TILE] = jnp.zeros((ROWS, TILE), F32)

    def entry(r, s):
        return jnp.clip(tabs[r, s], 0, TILE)

    def gather(c):
        def add(d):
            for k in range(SLOTS):
                s = d * 8 + k
                acc[s] = recv[c, d, k * ROWS:(k + 1) * ROWS, :] + acc[entry(0, s)]

        def one(d, _):
            plane_wait(c, d).wait_recv()
            add(d)
            return 0

        add(0)
        lax.fori_loop(1, PLANE, one, 0)
        for dy in range(SIDE):
            group = lax.rem(y + dy, SIDE) * 2
            for j in range(OWNED):
                other = entry(1, (group + 1 - core) * OWNED + j)
                csend[c, dy, j] = acc[other]
        core_copy(c).start()
        for dy in range(SIDE):
            group = lax.rem(y + dy, SIDE) * 2
            for j in range(OWNED):
                ysend[c, dy, j] = acc[entry(1, (group + core) * OWNED + j)]

    def spread(c):
        core_copy(c).wait_recv()
        for dy in (2, 1, 3, 0):
            ysend[c, dy] = ysend[c, dy] + crecv[c, dy]
            if dy:
                y_copy(c, dy).start()

    def total(c):
        for dy in range(1, SIDE):
            y_copy(c, dy).wait_recv()
        return (ysend[c, 0] + yrecv[c, 1]) + (yrecv[c, 2] + yrecv[c, 3])

    def weights(q, _):
        gather(q)
        spread(q)
        return 0

    lax.fori_loop(0, PARTS, weights, 0)

    def finish(q, _):
        value = total(PARTS + q) / (total(q) + 1.0)
        for j in range(OWNED):
            out[j, pl.ds(q * ROWS, ROWS), :] = value[j]
        return 0

    def pixels(q, _):
        gather(PARTS + q)
        spread(PARTS + q)
        return 0

    lax.fori_loop(0, PARTS, pixels, 0)
    lax.fori_loop(0, PARTS, finish, 0)

    def drain(c, _):
        def one(d, _):
            plane_wait(c, d).wait_send()
            return 0

        lax.fori_loop(1, PLANE, one, 0)
        core_copy(c).wait_send()
        for dy in range(1, SIDE):
            y_copy(c, dy).wait_send()
        return 0

    lax.fori_loop(0, CHUNKS, drain, 0)
    for d in range(1, PLANE):
        meta_copy(d).wait_send()


def shards(image, weight, coeffs, trim, destination, row_taps, col_taps):
    column = destination // OWNED % PLANE
    order = jnp.arange(COUNT, dtype=I32)
    earlier = (column[:, None] == column[None, :]) & (order[None, :] < order[:, None])
    slot = column * 8 + jnp.sum(earlier.astype(I32), axis=1)
    match = jnp.arange(PLANE * 8, dtype=I32)[:, None] == slot[None, :]
    perm = jnp.min(jnp.where(match, order[None, :], COUNT), axis=1)
    smem = pl.BlockSpec(memory_space=pltpu.SMEM)
    vmem = pl.BlockSpec(memory_space=pltpu.VMEM)
    dma = pltpu.SemaphoreType.DMA
    return pl.pallas_call(
        kernel,
        out_shape=jax.ShapeDtypeStruct((OWNED, TILE, TILE), F32),
        in_specs=[smem] * 6 + [vmem] * 2,
        out_specs=vmem,
        scratch_shapes=[
            pltpu.VMEM((COUNT + 1, TILE, TILE), F32),
            pltpu.VMEM((COUNT + 1, TILE, TILE), F32),
            pltpu.VMEM((2, NB * TILE // 2, 2 * TILE), BF16),
            pltpu.VMEM((NB * TILE, 2 * TILE), BF16),
            pltpu.VMEM((2, 2 * TILE, 2 * TILE), BF16),
            pltpu.VMEM((2 * QUAD * TILE, NB * TILE), BF16),
            pltpu.VMEM((CHUNKS, PLANE, SLOTS * ROWS, TILE), F32),
            pltpu.VMEM((CHUNKS, PLANE, SLOTS * ROWS, TILE), F32),
            pltpu.VMEM((TILE + 1, ROWS, TILE), F32),
            pltpu.VMEM((PLANE, 8, TILE), I32),
            pltpu.VMEM((PLANE, 8, TILE), I32),
            pltpu.VMEM((8, TILE), I32),
            pltpu.SMEM((8, TILE), I32),
            pltpu.VMEM((CHUNKS, SIDE, OWNED, ROWS, TILE), F32),
            pltpu.VMEM((CHUNKS, SIDE, OWNED, ROWS, TILE), F32),
            pltpu.VMEM((CHUNKS, SIDE, OWNED, ROWS, TILE), F32),
            pltpu.VMEM((CHUNKS, SIDE, OWNED, ROWS, TILE), F32),
            dma((CHUNKS, PLANE)),
            dma((CHUNKS, PLANE)),
            dma((PLANE,)),
            dma((PLANE,)),
            dma((CHUNKS,)),
            dma((CHUNKS,)),
            dma((CHUNKS, SIDE)),
            dma((CHUNKS, SIDE)),
            dma(()),
        ],
        compiler_params=pltpu.CompilerParams(
            collective_id=0, has_side_effects=True, vmem_limit_bytes=60 << 20
        ),
        name="coadd",
    )(perm, destination, trim, coeffs, row_taps, col_taps, image, weight)


def solution(mesh):
    placed = (
        P(("visit", "patch"), None, None),
        P(("visit", "patch"), None, None),
        P(("visit", "patch"), None),
        P(("visit", "patch"), None),
        P(("visit", "patch")),
        P(),
        P(),
    )
    return jax.shard_map(
        shards,
        mesh=mesh,
        in_specs=placed,
        out_specs=P(("visit", "patch"), None, None),
        check_vma=False,
    )
```

time: 597 us -> 148 us (0.25)
  matrix products: 258 us -> 0 us
  waiting for transfers between devices: 203 us -> 0 us
  Pallas kernels: 0 us -> 141 us
  local copies, waits for them, and re-layouts: 59.3 us -> 4.61 us
  starting transfers between devices: 22.3 us -> 0 us
  other arithmetic: 19.4 us -> 2.12 us
  loops' own time: 15.8 us -> 0 us
  between operations: 14 us -> 0.01 us
    dot_general x23 -> x0, matrix products: 258 us -> none  [the longest x10 146 us: one(): return jnp.einsum('kmi,kil->ml', row_band, across, precision=HIGH)]
    all_to_all x3 -> x0, waiting for transfers between devices: 148 us -> none  [the longest x1 148 us: shards(): lax.all_to_all(sent, 'patch', split_axis=0, concat_axis=0, tiled=True)]
    pallas_call x0 -> x1, Pallas kernels: none -> 141 us  [shards(): pl.pallas_call(kernel, out_shape=jax.ShapeDtypeStruct((OWNED, TILE, TILE)...]
    reduce_scatter x1 -> x0, waiting for transfers between devices: 54.8 us -> none  [shards(): lax.psum_scatter(column_sum, 'visit', scatter_dimension=0, tiled=True)]
    all_to_all x3 -> x0, starting transfers between devices: 22.3 us -> none  [the longest x1 8.43 us: shards(): lax.all_to_all(slot_row, 'patch', split_axis=0, concat_axis=0, tiled=True)]
    another operation x1 -> x0, loops' own time: 15.8 us -> none  [match_tiles(): return lax.map(one, (tiles, weights), batch_size=8)]
    reshape x2 -> x0, local copies, waits for them, and re-layouts: 12.2 us -> none  [the longest x1 11.6 us: shards(): received.reshape(-1, 2 * tile * tile)]
    slice x4 -> x0, local copies, waits for them, and re-layouts: 10.9 us -> none  [the longest x1 9.65 us: shards(): pixels[:, :, 0].reshape(-1, tile, tile)]
  transfers between devices with their start and end apart: 4 -> 0, of which waited for: 2 -> 0; matrix products, arithmetic and copies ran while one was open for 5% -> 0% of each run, Pallas kernels for 0% -> 0%
where the time goes in v1:
time: 148 us
  Pallas kernels  141 us (95%)
  local copies, waits for them, and re-layouts  4.61 us (3%)
  other arithmetic  2.12 us (1%)
    pallas_call x1, Pallas kernels, shards(): pl.pallas_call(kernel, out_shape=jax.ShapeDtypeStruct((OWNED, TILE, TILE)...  141 us
    unnamed x3, local copies, waits for them, and re-layouts  4.61 us

profile of v1, /device:TPU:1, one launch (start us, length us, event | category | flops | bytes accessed | tf_op | source)
XLA Modules:
  0.0 148.0 jit_solution(3961849418808932844)
XLA Ops:
  0.0 0.7 and_select_fusion
  0.7 0.2 convert_reduce_fusion
  0.9 0.7 multiply_add_fusion
  1.5 0.6 select_reduce_fusion.perm
  2.1 1.4 copy.11.coef
  3.5 1.4 copy.10.trim
  4.9 141.3 %coadd.1 = f32[8,128,128]{2,1,0:T(8,128)} custom-call(s32[128]{0:T(128)} %select_reduce_fusion.perm, s32[32]{0:T(128)} %dest.1, s32[32,4]{1,0:T(8,128)} %copy.10.trim, f32[32,16]{1,0:T(8,128)} %copy.11.coef, f32[16,21]{1,0:T(8,128)} %rtap.1, f32[16,21]{1,0:T(8,128)} %ctap.1, f32[32,128,128]{2,1,0:T(8,128)} %img.1, f32[32,128,128]{2,1,0:T(8,128)} %wgt.1), custom_call_target="tpu_custom_call" | custom-call | tf_op jit(solution)/shard_map/coadd/pallas_call | solution.py:318
  146.2 1.9 %copy.13 = f32[8,128,128]{2,1,0:T(8,128)} copy(f32[8,128,128]{2,1,0:T(8,128)} %coadd.1) | data formatting | bytes 1048576

commit v2 on v1

v2 whole, which is shorter than its diff:
```python
import jax
import jax.numpy as jnp
from jax import lax
from jax.experimental import pallas as pl
from jax.experimental.pallas import tpu as pltpu
from jax.sharding import PartitionSpec as P

MESH = pl.DeviceIdType.MESH
F32 = jnp.float32
BF16 = jnp.bfloat16
I32 = jnp.int32

TILE = 128
TAPS = 21
NB = 16
COUNT = 32
OWNED = 8
SLOTS = 5
WINDOW = 80
QUAD = 4

WEIGHT_GROUPS = ((0, 32, 4),)
PIXEL_GROUPS = ((0, 32, 3), (96, 16, 1), (112, 8, 2))
WEIGHT_CHUNKS = sum(g[2] for g in WEIGHT_GROUPS)
CHUNKS = WEIGHT_CHUNKS + sum(g[2] for g in PIXEL_GROUPS)
MOST = 32

SHIFTS = (
    (0, 0),
    (2, 2),
    (1, 2), (2, 1), (3, 2), (2, 3),
    (2, 0), (0, 2),
    (1, 1), (3, 3),
    (1, 3), (3, 1),
    (0, 1), (1, 0), (0, 3), (3, 0),
)
SIDE = 4
PLANE = len(SHIFTS)
Y_ORDER = (2, 1, 3, 0)


class Chunk:
    def __init__(self, c, start, rows, base):
        self.c, self.start, self.rows = c, start, rows
        self.at = base + start

    def slots(self, d):
        return d, pl.ds(pl.multiple_of(self.at * SLOTS, 8), self.rows * SLOTS), slice(None)

    def slot(self, d, k):
        return d, pl.ds(pl.multiple_of(self.at * SLOTS + k * self.rows, 8), self.rows), slice(None)

    def eight(self, dy):
        first = self.at * SIDE * OWNED + dy * OWNED * self.rows
        return pl.ds(pl.multiple_of(first, 8), OWNED * self.rows), slice(None)

    def one(self, dy, j):
        first = self.at * SIDE * OWNED + (dy * OWNED + j) * self.rows
        return pl.ds(pl.multiple_of(first, 8), self.rows), slice(None)


def kernel(
    dest, trim, coef, rtap, ctap, img_hbm, wgt_hbm, out_hbm,
    img, wgt, res, kept, nums, rl, cc, xr, wsp, send, recv, acc, msend, mrecv,
    permv, perms, tabv, tabs, csend, crecv, ysend, yrecv,
    i_sem, w_sem, o_sem, s_sem, r_sem, ms_sem, mr_sem, cs_sem, cr_sem, ys_sem, yr_sem, t_sem,
):
    visit, patch = lax.axis_index("visit"), lax.axis_index("patch")
    y, core = visit // 2, visit % 2
    z, x = patch // SIDE, patch % SIDE

    def column(d):
        dz, dx = SHIFTS[d]
        return lax.rem(z + dz, SIDE) * SIDE + lax.rem(x + dx, SIDE)

    def in_y(dy):
        return lax.rem(y + dy, SIDE) * 2 + core

    load_weight = pltpu.make_async_copy(wgt_hbm, wgt, w_sem)
    load_weight.start()
    load_image = pltpu.make_async_copy(img_hbm, img, i_sem)
    load_image.start()

    partners = [(visit, column(d)) for d in range(1, PLANE)]
    partners += [(visit + 1 - 2 * core, patch)]
    partners += [(in_y(dy), patch) for dy in range(1, SIDE)]
    barrier = pltpu.get_barrier_semaphore()
    for partner in partners:
        pl.semaphore_signal(barrier, inc=1, device_id=partner, device_id_type=MESH)

    row_of = lax.broadcasted_iota(I32, (TILE, TILE), 0)
    lane_of = lax.broadcasted_iota(I32, (TILE, TILE), 1)
    sub_of = lax.broadcasted_iota(I32, (8, TILE), 0)

    rows_c, lanes_c = row_of[:COUNT], lane_of[:COUNT]
    by_row = jnp.zeros((COUNT, TILE), I32)
    by_lane = jnp.full((COUNT, TILE), -1, I32)
    for n in range(COUNT):
        place = dest[n] // OWNED % PLANE
        by_row = jnp.where(rows_c == n, place, by_row)
        by_lane = jnp.where(lanes_c == n, place, by_lane)
    earlier = (by_row == by_lane) & (lanes_c < rows_c)
    rank = jnp.sum(earlier.astype(I32), axis=1, keepdims=True)
    tile_of = jnp.where(by_row * 8 + rank == lanes_c, rows_c, COUNT)
    permv[...] = jnp.broadcast_to(jnp.min(tile_of, axis=0, keepdims=True), (8, TILE))
    move = pltpu.make_async_copy(permv, perms, t_sem)
    move.start()

    load_weight.wait()

    def keep(n, _):
        inside = (row_of >= trim[0, n]) & (row_of < TILE - trim[1, n])
        inside &= (lane_of >= trim[2, n]) & (lane_of < TILE - trim[3, n])
        kept[n] = jnp.where(inside, wgt[n], 0.0)
        return 0

    lax.fori_loop(0, COUNT, keep, 0)
    kept[COUNT] = jnp.zeros((TILE, TILE), F32)
    nums[COUNT] = jnp.zeros((TILE, TILE), F32)
    move.wait()

    def tile_in(d, k):
        return jnp.clip(perms[0, column(d) * 8 + k], 0, COUNT)

    def remote(src, dst, send_sem, recv_sem, to):
        return pltpu.make_async_remote_copy(
            src_ref=src, dst_ref=dst, send_sem=send_sem, recv_sem=recv_sem,
            device_id=to, device_id_type=MESH,
        )

    def meta_copy(d):
        return remote(msend.at[d], mrecv.at[d], ms_sem.at[d], mr_sem.at[d], (visit, column(d)))

    def plane_copy(chunk, d, to):
        part = chunk.slots(d)
        c = chunk.c
        return remote(send.at[part], recv.at[part], s_sem.at[c, d], r_sem.at[c, d], (visit, to))

    def core_copy(chunk, dy):
        part = chunk.eight(dy)
        to = (visit + 1 - 2 * core, patch)
        c = chunk.c
        return remote(csend.at[part], crecv.at[part], cs_sem.at[c, dy], cr_sem.at[c, dy], to)

    def y_copy(chunk, dy):
        part = chunk.eight(dy)
        c = chunk.c
        to = (in_y(dy), patch)
        return remote(ysend.at[part], yrecv.at[part], ys_sem.at[c, dy], yr_sem.at[c, dy], to)

    def fill(source, chunk, d):
        target = recv if d == 0 else send
        for k in range(SLOTS):
            block = source[tile_in(d, k), pl.ds(chunk.start, chunk.rows), :]
            target[chunk.slot(d, k)] = block

    def send_chunk(source, chunk):
        for d in range(1, PLANE):
            fill(source, chunk, d)
            plane_copy(chunk, d, column(d)).start()
        fill(source, chunk, 0)

    def loop(groups, c, base, first, body):
        for start, rows, count in groups:

            def one(q, _, start=start, rows=rows, c=c):
                body(Chunk(c + q, start + q * rows, rows, base))
                return 0

            begin = min(first, count)
            lax.fori_loop(begin, count, one, 0)
            first -= begin
            c += count

    weight_args = (WEIGHT_GROUPS, 0, 0)
    pixel_args = (PIXEL_GROUPS, WEIGHT_CHUNKS, TILE)

    pl.semaphore_wait(barrier, len(partners))
    send_chunk(kept, Chunk(0, 0, WEIGHT_GROUPS[0][1], 0))
    for d in range(PLANE):
        rows = jnp.full((8, TILE), -1, I32)
        for k in range(SLOTS):
            n = tile_in(d, k)
            to = dest[jnp.minimum(n, COUNT - 1)]
            row = jnp.where(n < COUNT, to // (OWNED * PLANE) * OWNED + to % OWNED, -1)
            rows = jnp.where(sub_of == k, row, rows)
        if d == 0:
            mrecv[0] = rows
        else:
            msend[d] = rows
            meta_copy(d).start()
    loop(*weight_args, 1, lambda chunk: send_chunk(kept, chunk))

    half_row = lax.broadcasted_iota(I32, (TILE // 2, 2 * TILE), 0)
    half_lane = lax.broadcasted_iota(I32, (TILE // 2, 2 * TILE), 1)
    piece = (half_lane >= WINDOW).astype(I32) + (half_lane >= 2 * WINDOW).astype(I32)
    place = half_lane - piece * WINDOW

    def tables(k, _):
        for h in range(2):
            offset = place + h * (TILE - WINDOW) - half_row - h * (TILE // 2) + TAPS // 2
            offset = jnp.where(half_lane < 3 * WINDOW, offset, -1)
            taps = jnp.zeros((TILE // 2, 2 * TILE), F32)
            for index in range(TAPS):
                taps = jnp.where(offset == index, rtap[k, index], taps)
            high = taps.astype(BF16).astype(F32)
            rl[h, pl.ds(k * (TILE // 2), TILE // 2), :] = jnp.where(
                piece == 2, taps - high, high
            ).astype(BF16)
        offset = row_of - lane_of + TAPS // 2
        taps = jnp.zeros((TILE, TILE), F32)
        for index in range(TAPS):
            taps = jnp.where(offset == index, ctap[k, index], taps)
        high = taps.astype(BF16)
        cc[pl.ds(k * TILE, TILE), 0:TILE] = high
        cc[pl.ds(k * TILE, TILE), TILE:] = (taps - high.astype(F32)).astype(BF16)
        return 0

    lax.fori_loop(0, NB, tables, 0)
    load_image.wait()
    for h in range(2):
        xr[h, 3 * WINDOW:, :] = jnp.zeros((2 * TILE - 3 * WINDOW, 2 * TILE), BF16)

    def match(i, _):
        for pair in range(QUAD // 2):
            for u in range(2):
                pixels = img[i * QUAD + pair * 2 + u]
                high = pixels.astype(BF16)
                low = (pixels - high.astype(F32)).astype(BF16)
                lanes = slice(u * TILE, (u + 1) * TILE)
                for h in range(2):
                    a = h * (TILE - WINDOW)
                    xr[h, 0:WINDOW, lanes] = high[a:a + WINDOW]
                    xr[h, WINDOW:2 * WINDOW, lanes] = low[a:a + WINDOW]
                    xr[h, 2 * WINDOW:3 * WINDOW, lanes] = high[a:a + WINDOW]
            for h in range(2):
                for g in range(0, NB, 4):
                    down = jnp.dot(
                        rl[h, g * (TILE // 2):(g + 4) * (TILE // 2), :], xr[h],
                        preferred_element_type=F32,
                    )
                    for k in range(g, g + 4):
                        for u in range(2):
                            t = pair * 2 + u
                            b = (k - g) * (TILE // 2)
                            w = down[b:b + TILE // 2, u * TILE:(u + 1) * TILE]
                            w = w * coef[k, i * QUAD + t]
                            high = w.astype(BF16)
                            r = t * TILE + h * (TILE // 2)
                            lanes = slice(k * TILE, (k + 1) * TILE)
                            wsp[r:r + TILE // 2, lanes] = high
                            r += QUAD * TILE
                            wsp[r:r + TILE // 2, lanes] = (w - high.astype(F32)).astype(BF16)
        both = jnp.dot(wsp[...], cc[...], preferred_element_type=F32)
        both = both[:, :TILE] + both[:, TILE:]
        for t in range(QUAD):
            n = i * QUAD + t
            matched = both[t * TILE:(t + 1) * TILE]
            matched = matched + both[(QUAD + t) * TILE:(QUAD + t + 1) * TILE]
            nums[n] = kept[n] * matched
        return 0

    lax.fori_loop(0, COUNT // QUAD, match, 0)
    loop(*pixel_args, 0, lambda chunk: send_chunk(nums, chunk))

    for d in range(1, PLANE):
        meta_copy(d).wait()
    along = mrecv[...].reshape(TILE, TILE)
    across = along.T
    before = jnp.where((along == across) & (row_of < lane_of), row_of, -1)
    before = jnp.max(before, axis=0, keepdims=True)
    last = jnp.max(jnp.where(along == lane_of, row_of, -1), axis=0, keepdims=True)
    table = jnp.where(sub_of == 0, before, last)
    tabv[...] = jnp.where(table < 0, TILE, table)
    move = pltpu.make_async_copy(tabv, tabs, t_sem)
    move.start()
    move.wait()
    acc[TILE] = jnp.zeros((MOST, TILE), F32)

    def entry(r, s):
        return jnp.clip(tabs[r, s], 0, TILE)

    def gather(chunk):
        rows = chunk.rows

        def add(d):
            for k in range(SLOTS):
                s = d * 8 + k
                acc[s, :rows] = recv[chunk.slot(d, k)] + acc[entry(0, s), :rows]

        def one(d, _):
            plane_copy(chunk, d, column(1)).wait_recv()
            add(d)
            return 0

        add(0)
        lax.fori_loop(1, PLANE, one, 0)
        for dy in Y_ORDER:
            group = lax.rem(y + dy, SIDE) * 2
            for j in range(OWNED):
                csend[chunk.one(dy, j)] = acc[entry(1, (group + 1 - core) * OWNED + j), :rows]
            core_copy(chunk, dy).start()
        for dy in Y_ORDER:
            group = lax.rem(y + dy, SIDE) * 2
            for j in range(OWNED):
                ysend[chunk.one(dy, j)] = acc[entry(1, (group + core) * OWNED + j), :rows]

    def spread(chunk):
        for dy in Y_ORDER:
            part = chunk.eight(dy)
            core_copy(chunk, dy).wait_recv()
            ysend[part] = ysend[part] + crecv[part]
            if dy:
                y_copy(chunk, dy).start()

    def drain(chunk):
        def one(d, _):
            plane_copy(chunk, d, column(1)).wait_send()
            return 0

        lax.fori_loop(1, PLANE, one, 0)
        for dy in range(SIDE):
            core_copy(chunk, dy).wait_send()
            if dy:
                y_copy(chunk, dy).wait_send()

    def total(chunk):
        for dy in range(1, SIDE):
            y_copy(chunk, dy).wait_recv()
        a, b, c, d = (chunk.eight(dy) for dy in range(SIDE))
        return (ysend[a] + yrecv[b]) + (yrecv[c] + yrecv[d])

    def weights(chunk):
        gather(chunk)
        spread(chunk)

    def sums(chunk):
        value = total(chunk) + 1.0
        for j in range(OWNED):
            block = value[j * chunk.rows:(j + 1) * chunk.rows]
            res[j, pl.ds(chunk.start, chunk.rows), :] = block

    def finish(chunk):
        value = total(chunk)
        for j in range(OWNED):
            part = (j, pl.ds(chunk.start, chunk.rows), slice(None))
            res[part] = value[j * chunk.rows:(j + 1) * chunk.rows] / res[part]

    def store(chunk):
        part = (slice(None), pl.ds(chunk.start, chunk.rows), slice(None))
        return pltpu.make_async_copy(res.at[part], out_hbm.at[part], o_sem.at[chunk.c])

    loop(*weight_args, 0, weights)
    loop(*weight_args, 0, sums)
    loop(*weight_args, 0, drain)

    pixel_chunks = []
    c = WEIGHT_CHUNKS
    for start, rows, count in PIXEL_GROUPS:
        for q in range(count):
            pixel_chunks.append(Chunk(c, start + q * rows, rows, TILE))
            c += 1
    for index, chunk in enumerate(pixel_chunks):
        gather(chunk)
        spread(chunk)
        if index:
            finish(pixel_chunks[index - 1])
            store(pixel_chunks[index - 1]).start()
        if index > 1:
            drain(pixel_chunks[index - 2])
    finish(pixel_chunks[-1])
    store(pixel_chunks[-1]).start()
    for chunk in pixel_chunks[-2:]:
        drain(chunk)
    for chunk in pixel_chunks:
        store(chunk).wait()


def shards(image, weight, coeffs, trim, destination, row_taps, col_taps):
    smem = pl.BlockSpec(memory_space=pltpu.SMEM)
    hbm = pl.BlockSpec(memory_space=pl.ANY)
    dma = pltpu.SemaphoreType.DMA
    stack = 2 * TILE * SIDE * OWNED
    return pl.pallas_call(
        kernel,
        out_shape=jax.ShapeDtypeStruct((OWNED, TILE, TILE), F32),
        in_specs=[smem] * 5 + [hbm] * 2,
        out_specs=hbm,
        scratch_shapes=[
            pltpu.VMEM((COUNT, TILE, TILE), F32),
            pltpu.VMEM((COUNT, TILE, TILE), F32),
            pltpu.VMEM((OWNED, TILE, TILE), F32),
            pltpu.VMEM((COUNT + 1, TILE, TILE), F32),
            pltpu.VMEM((COUNT + 1, TILE, TILE), F32),
            pltpu.VMEM((2, NB * TILE // 2, 2 * TILE), BF16),
            pltpu.VMEM((NB * TILE, 2 * TILE), BF16),
            pltpu.VMEM((2, 2 * TILE, 2 * TILE), BF16),
            pltpu.VMEM((2 * QUAD * TILE, NB * TILE), BF16),
            pltpu.VMEM((PLANE, 2 * TILE * SLOTS, TILE), F32),
            pltpu.VMEM((PLANE, 2 * TILE * SLOTS, TILE), F32),
            pltpu.VMEM((TILE + 1, MOST, TILE), F32),
            pltpu.VMEM((PLANE, 8, TILE), I32),
            pltpu.VMEM((PLANE, 8, TILE), I32),
            pltpu.VMEM((8, TILE), I32),
            pltpu.SMEM((8, TILE), I32),
            pltpu.VMEM((8, TILE), I32),
            pltpu.SMEM((8, TILE), I32),
            pltpu.VMEM((stack, TILE), F32),
            pltpu.VMEM((stack, TILE), F32),
            pltpu.VMEM((stack, TILE), F32),
            pltpu.VMEM((stack, TILE), F32),
            dma(()),
            dma(()),
            dma((CHUNKS,)),
            dma((CHUNKS, PLANE)),
            dma((CHUNKS, PLANE)),
            dma((PLANE,)),
            dma((PLANE,)),
            dma((CHUNKS, SIDE)),
            dma((CHUNKS, SIDE)),
            dma((CHUNKS, SIDE)),
            dma((CHUNKS, SIDE)),
            dma(()),
        ],
        compiler_params=pltpu.CompilerParams(
            collective_id=0, has_side_effects=True, vmem_limit_bytes=60 << 20
        ),
        name="coadd",
    )(destination, trim.T, coeffs.T, row_taps, col_taps, image, weight)


def solution(mesh):
    placed = (
        P(("visit", "patch"), None, None),
        P(("visit", "patch"), None, None),
        P(("visit", "patch"), None),
        P(("visit", "patch"), None),
        P(("visit", "patch")),
        P(),
        P(),
    )
    return jax.shard_map(
        shards,
        mesh=mesh,
        in_specs=placed,
        out_specs=P(("visit", "patch"), None, None),
        check_vma=False,
    )
```

time: 148 us -> 140 us (0.946)
  Pallas kernels: 141 us -> 138 us
  local copies, waits for them, and re-layouts: 4.61 us -> 1.87 us
  other arithmetic: 2.12 us -> 0 us
    pallas_call x1, Pallas kernels: 141 us -> 138 us  [shards(): pl.pallas_call(kernel, out_shape=jax.ShapeDtypeStruct((OWNED, TILE, TILE)...]
    unnamed x3 -> x1, local copies, waits for them, and re-layouts: 4.61 us -> 1.87 us
where the time goes in v2:
time: 140 us
  Pallas kernels  138 us (99%)
  local copies, waits for them, and re-layouts  1.87 us (1%)
    pallas_call x1, Pallas kernels, shards(): pl.pallas_call(kernel, out_shape=jax.ShapeDtypeStruct((OWNED, TILE, TILE)...  138 us

profile of v2, /device:TPU:1, one launch (start us, length us, event | category | flops | bytes accessed | tf_op | source)
XLA Modules:
  0.0 139.9 jit_solution(16307919880465567686)
XLA Ops:
  0.0 138.1 %coadd.1 = f32[8,128,128]{2,1,0:T(8,128)} custom-call(s32[32]{0:T(128)} %dest.1, s32[4,32]{1,0:T(4,128)} %bitcast.3, f32[16,32]{1,0:T(8,128)} %bitcast.2, f32[16,21]{1,0:T(8,128)} %rtap.1, f32[16,21]{1,0:T(8,128)} %ctap.1, f32[32,128,128]{2,1,0:T(8,128)} %img_hbm.1, f32[32,128,128]{2,1,0:T(8,128)} %wgt_hbm.1), custom_call_target="tpu_custom_call" | custom-call | tf_op jit(solution)/shard_map/coadd/pallas_call | solution.py:384
  138.1 1.9 %copy.9 = f32[8,128,128]{2,1,0:T(8,128)} copy(f32[8,128,128]{2,1,0:T(8,128)} %coadd.1) | data formatting | bytes 1048576

commit v3 on v2

--- a/solution.py
+++ b/solution.py
@@ -60,10 +60,10 @@
 
 
 def kernel(
-    dest, trim, coef, rtap, ctap, img_hbm, wgt_hbm, out_hbm,
-    img, wgt, res, kept, nums, rl, cc, xr, wsp, send, recv, acc, msend, mrecv,
+    dest, trim, coef, rtap, ctap, img_hbm, wgt_hbm, res,
+    img, wgt, kept, nums, rl, cc, xr, wsp, send, recv, acc, msend, mrecv,
     permv, perms, tabv, tabs, csend, crecv, ysend, yrecv,
-    i_sem, w_sem, o_sem, s_sem, r_sem, ms_sem, mr_sem, cs_sem, cr_sem, ys_sem, yr_sem, t_sem,
+    i_sem, w_sem, s_sem, r_sem, ms_sem, mr_sem, cs_sem, cr_sem, ys_sem, yr_sem, t_sem,
 ):
     visit, patch = lax.axis_index("visit"), lax.axis_index("patch")
     y, core = visit // 2, visit % 2
@@ -76,8 +76,14 @@
     def in_y(dy):
         return lax.rem(y + dy, SIDE) * 2 + core
 
-    load_weight = pltpu.make_async_copy(wgt_hbm, wgt, w_sem)
-    load_weight.start()
+    part_rows = WEIGHT_GROUPS[0][1]
+
+    def load_weight(q):
+        part = (slice(None), pl.ds(q * part_rows, part_rows), slice(None))
+        return pltpu.make_async_copy(wgt_hbm.at[part], wgt.at[part], w_sem.at[q])
+
+    for q in range(WEIGHT_CHUNKS):
+        load_weight(q).start()
     load_image = pltpu.make_async_copy(img_hbm, img, i_sem)
     load_image.start()
 
@@ -96,7 +102,7 @@
     by_row = jnp.zeros((COUNT, TILE), I32)
     by_lane = jnp.full((COUNT, TILE), -1, I32)
     for n in range(COUNT):
-        place = dest[n] // OWNED % PLANE
+        place = (dest[n] >> 3) & (PLANE - 1)
         by_row = jnp.where(rows_c == n, place, by_row)
         by_lane = jnp.where(lanes_c == n, place, by_lane)
     earlier = (by_row == by_lane) & (lanes_c < rows_c)
@@ -106,15 +112,22 @@
     move = pltpu.make_async_copy(permv, perms, t_sem)
     move.start()
 
-    load_weight.wait()
-
-    def keep(n, _):
-        inside = (row_of >= trim[0, n]) & (row_of < TILE - trim[1, n])
-        inside &= (lane_of >= trim[2, n]) & (lane_of < TILE - trim[3, n])
-        kept[n] = jnp.where(inside, wgt[n], 0.0)
-        return 0
-
-    lax.fori_loop(0, COUNT, keep, 0)
+    rows_p, lanes_p = row_of[:part_rows], lane_of[:part_rows]
+
+    def keep(chunk):
+        load_weight(chunk.c).wait()
+        rows_here = rows_p + chunk.start
+        part = pl.ds(chunk.start, chunk.rows)
+
+        def one(n, _):
+            inside = (rows_here >= trim[0, n]) & (rows_here < TILE - trim[1, n])
+            inside &= (lanes_p >= trim[2, n]) & (lanes_p < TILE - trim[3, n])
+            kept[n, part, :] = jnp.where(inside, wgt[n, part, :], 0.0)
+            return 0
+
+        lax.fori_loop(0, COUNT, one, 0)
+
+    keep(Chunk(0, 0, part_rows, 0))
     kept[COUNT] = jnp.zeros((TILE, TILE), F32)
     nums[COUNT] = jnp.zeros((TILE, TILE), F32)
     move.wait()
@@ -189,7 +202,12 @@
         else:
             msend[d] = rows
             meta_copy(d).start()
-    loop(*weight_args, 1, lambda chunk: send_chunk(kept, chunk))
+
+    def weigh(chunk):
+        keep(chunk)
+        send_chunk(kept, chunk)
+
+    loop(*weight_args, 1, weigh)
 
     half_row = lax.broadcasted_iota(I32, (TILE // 2, 2 * TILE), 0)
     half_lane = lax.broadcasted_iota(I32, (TILE // 2, 2 * TILE), 1)
@@ -346,10 +364,6 @@
             part = (j, pl.ds(chunk.start, chunk.rows), slice(None))
             res[part] = value[j * chunk.rows:(j + 1) * chunk.rows] / res[part]
 
-    def store(chunk):
-        part = (slice(None), pl.ds(chunk.start, chunk.rows), slice(None))
-        return pltpu.make_async_copy(res.at[part], out_hbm.at[part], o_sem.at[chunk.c])
-
     loop(*weight_args, 0, weights)
     loop(*weight_args, 0, sums)
     loop(*weight_args, 0, drain)
@@ -365,15 +379,11 @@
         spread(chunk)
         if index:
             finish(pixel_chunks[index - 1])
-            store(pixel_chunks[index - 1]).start()
         if index > 1:
             drain(pixel_chunks[index - 2])
     finish(pixel_chunks[-1])
-    store(pixel_chunks[-1]).start()
     for chunk in pixel_chunks[-2:]:
         drain(chunk)
-    for chunk in pixel_chunks:
-        store(chunk).wait()
 
 
 def shards(image, weight, coeffs, trim, destination, row_taps, col_taps):
@@ -383,13 +393,12 @@
     stack = 2 * TILE * SIDE * OWNED
     return pl.pallas_call(
         kernel,
-        out_shape=jax.ShapeDtypeStruct((OWNED, TILE, TILE), F32),
+        out_shape=pltpu.VMEM((OWNED, TILE, TILE), F32),
         in_specs=[smem] * 5 + [hbm] * 2,
-        out_specs=hbm,
+        out_specs=pl.BlockSpec(memory_space=pltpu.VMEM),
         scratch_shapes=[
             pltpu.VMEM((COUNT, TILE, TILE), F32),
             pltpu.VMEM((COUNT, TILE, TILE), F32),
-            pltpu.VMEM((OWNED, TILE, TILE), F32),
             pltpu.VMEM((COUNT + 1, TILE, TILE), F32),
             pltpu.VMEM((COUNT + 1, TILE, TILE), F32),
             pltpu.VMEM((2, NB * TILE // 2, 2 * TILE), BF16),
@@ -410,8 +419,7 @@
             pltpu.VMEM((stack, TILE), F32),
             pltpu.VMEM((stack, TILE), F32),
             dma(()),
-            dma(()),
-            dma((CHUNKS,)),
+            dma((WEIGHT_CHUNKS,)),
             dma((CHUNKS, PLANE)),
             dma((CHUNKS, PLANE)),
             dma((PLANE,)),

time: 140 us -> 138 us (0.986)
  no operation moved by 1% of the time
where the time goes in v3:
time: 138 us
  Pallas kernels  137 us (99%)
    pallas_call x1, Pallas kernels, shards(): pl.pallas_call(kernel, out_shape=pltpu.VMEM((OWNED, TILE, TILE), F32), in...  137 us

profile of v3, /device:TPU:1, one launch (start us, length us, event | category | flops | bytes accessed | tf_op | source)
XLA Modules:
  0.0 138.0 jit_solution(13696860016291295892)
XLA Ops:
  0.0 137.2 %coadd.1 = f32[8,128,128]{2,1,0:T(8,128)S(1)} custom-call(s32[32]{0:T(128)} %dest.1, s32[4,32]{1,0:T(4,128)} %bitcast.3, f32[16,32]{1,0:T(8,128)} %bitcast.2, f32[16,21]{1,0:T(8,128)} %rtap.1, f32[16,21]{1,0:T(8,128)} %ctap.1, f32[32,128,128]{2,1,0:T(8,128)} %img_hbm.1, f32[32,128,128]{2,1,0:T(8,128)} %wgt_hbm.1), custom_call_target="tpu_custom_call" | custom-call | tf_op jit(solution)/shard_map/coadd/pallas_call | solution.py:394
  137.2 0.8 copy.9

commit v4 on v3

--- a/solution.py
+++ b/solution.py
@@ -20,10 +20,10 @@
 QUAD = 4
 
 WEIGHT_GROUPS = ((0, 32, 4),)
-PIXEL_GROUPS = ((0, 32, 3), (96, 16, 1), (112, 8, 2))
+PIXEL_GROUPS = ((0, 40, 2), (80, 24, 1), (104, 16, 1), (120, 8, 1))
 WEIGHT_CHUNKS = sum(g[2] for g in WEIGHT_GROUPS)
 CHUNKS = WEIGHT_CHUNKS + sum(g[2] for g in PIXEL_GROUPS)
-MOST = 32
+MOST = 40
 
 SHIFTS = (
     (0, 0),
@@ -374,15 +374,19 @@
         for q in range(count):
             pixel_chunks.append(Chunk(c, start + q * rows, rows, TILE))
             c += 1
+    undrained = []
     for index, chunk in enumerate(pixel_chunks):
         gather(chunk)
         spread(chunk)
         if index:
             finish(pixel_chunks[index - 1])
-        if index > 1:
-            drain(pixel_chunks[index - 2])
+        if index + 1 == len(pixel_chunks):
+            break
+        undrained.append(chunk)
+        if index > 1 and index + 2 < len(pixel_chunks):
+            drain(undrained.pop(0))
     finish(pixel_chunks[-1])
-    for chunk in pixel_chunks[-2:]:
+    for chunk in undrained + pixel_chunks[-1:]:
         drain(chunk)
 
 

time: 138 us -> 136 us (0.986)
  Pallas kernels: 137 us -> 135 us
    pallas_call x1, Pallas kernels: 137 us -> 135 us  [shards(): pl.pallas_call(kernel, out_shape=pltpu.VMEM((OWNED, TILE, TILE), F32), in...]
where the time goes in v4:
time: 136 us
  Pallas kernels  135 us (99%)
    pallas_call x1, Pallas kernels, shards(): pl.pallas_call(kernel, out_shape=pltpu.VMEM((OWNED, TILE, TILE), F32), in...  135 us

profile of v4, /device:TPU:1, one launch (start us, length us, event | category | flops | bytes accessed | tf_op | source)
XLA Modules:
  0.0 136.3 jit_solution(17834651955134069003)
XLA Ops:
  0.0 135.5 %coadd.1 = f32[8,128,128]{2,1,0:T(8,128)S(1)} custom-call(s32[32]{0:T(128)} %dest.1, s32[4,32]{1,0:T(4,128)} %bitcast.3, f32[16,32]{1,0:T(8,128)} %bitcast.2, f32[16,21]{1,0:T(8,128)} %rtap.1, f32[16,21]{1,0:T(8,128)} %ctap.1, f32[32,128,128]{2,1,0:T(8,128)} %img_hbm.1, f32[32,128,128]{2,1,0:T(8,128)} %wgt_hbm.1), custom_call_target="tpu_custom_call" | custom-call | tf_op jit(solution)/shard_map/coadd/pallas_call | solution.py:398
  135.5 0.8 copy.9

commit v5 on v4

--- a/solution.py
+++ b/solution.py
@@ -28,11 +28,11 @@
 SHIFTS = (
     (0, 0),
     (2, 2),
-    (1, 2), (2, 1), (3, 2), (2, 3),
+    (3, 2), (2, 3), (1, 2), (2, 1),
     (2, 0), (0, 2),
+    (1, 3), (3, 1),
     (1, 1), (3, 3),
-    (1, 3), (3, 1),
-    (0, 1), (1, 0), (0, 3), (3, 0),
+    (0, 3), (3, 0), (0, 1), (1, 0),
 )
 SIDE = 4
 PLANE = len(SHIFTS)

time: 136 us -> 136 us (level)
  no operation moved by 1% of the time
where the time goes in v5:
time: 136 us; the launch traced here: 135 us
  Pallas kernels  134 us (99%)
    pallas_call x1, Pallas kernels, shards(): pl.pallas_call(kernel, out_shape=pltpu.VMEM((OWNED, TILE, TILE), F32), in...  134 us

profile of v5, /device:TPU:1, one launch (start us, length us, event | category | flops | bytes accessed | tf_op | source)
XLA Modules:
  0.0 135.1 jit_solution(6783046920003098151)
XLA Ops:
  0.0 134.3 %coadd.1 = f32[8,128,128]{2,1,0:T(8,128)S(1)} custom-call(s32[32]{0:T(128)} %dest.1, s32[4,32]{1,0:T(4,128)} %bitcast.3, f32[16,32]{1,0:T(8,128)} %bitcast.2, f32[16,21]{1,0:T(8,128)} %rtap.1, f32[16,21]{1,0:T(8,128)} %ctap.1, f32[32,128,128]{2,1,0:T(8,128)} %img_hbm.1, f32[32,128,128]{2,1,0:T(8,128)} %wgt_hbm.1), custom_call_target="tpu_custom_call" | custom-call | tf_op jit(solution)/shard_map/coadd/pallas_call | solution.py:398
  134.3 0.8 copy.9
